TPU v7x, 32 devices: a whole 2x2x4 slice. The times are simulated.
32 devices in a mesh: groups: 2 (over y), blk: 4 (over z), red: 2 (over x), sub: 2 (over core).
Axes of the slice: x: 2, y: 2, z: 4, core: 2. Of those that a mesh axis runs over, the one named last changes fastest.
Arguments:
- tokens: bfloat16 [256, 8192], P(('groups', 'blk'), ('red', 'sub')), parts along dimension 0, may hold values from -6 to 6
- gate_weight: bfloat16 [8192, 16384], P(('red', 'sub'), 'blk'), may hold values from -0.09375 to 0.09375
- up_weight: bfloat16 [8192, 16384], P(('red', 'sub'), 'blk'), may hold values from -0.09375 to 0.09375
- down_weight: bfloat16 [16384, 8192], P('blk', ('red', 'sub')), may hold values from -0.125 to 0.125
- in_mask: int32 [64, 128], P(('red', 'sub'), 'blk'), may hold values 0 or 1
- out_mask: int32 [128, 64], P('blk', ('red', 'sub')), may hold values 0 or 1
Outputs:
- mixed: bfloat16 [256, 8192], P(('groups', 'blk'), ('red', 'sub')), parts along dimension 0
There are 2 independent parts, one for each index of `groups`. A program takes and returns all parts, laid end to end along the dimension named above; an argument that names none is the same for every part. Nothing has to cross between parts.
All inputs are finite; a program needn't handle non-finite values. No bound on the sum of `in_mask` or of `out_mask` on one device may be relied on, other than what follows from the above.
Results may differ from a plain program's by a relative error of at most 0.02.
Values may be sent and summed in bfloat16 or wider, within the bound.
A program may use at most 192 MiB of HBM per device.

v0:
```python
import jax
import jax.numpy as jnp
from jax import lax
from jax.sharding import PartitionSpec as P


def expand_blocks(weight, block_mask):
    row_count, col_count = weight.shape
    mask_rows, mask_cols = block_mask.shape
    shaped = weight.reshape(mask_rows, row_count // mask_rows, mask_cols, col_count // mask_cols)
    kept_blocks = (block_mask == 1)[:, None, :, None]
    return jnp.where(kept_blocks, shaped, jnp.zeros_like(shaped)).reshape(row_count, col_count)


def per_device(tokens, gate_weight, up_weight, down_weight, in_mask, out_mask):
    paired = jnp.concatenate(
        [expand_blocks(gate_weight, in_mask), expand_blocks(up_weight, in_mask)], axis=1
    )
    down_kept = expand_blocks(down_weight, out_mask)
    unit_width = gate_weight.shape[1]
    partial_units = jnp.dot(
        lax.all_gather(tokens, "blk", axis=0, tiled=True),
        paired,
        preferred_element_type=jnp.float32,
    )
    owned = lax.psum_scatter(
        partial_units.astype(jnp.bfloat16), ("red", "sub"), scatter_dimension=0, tiled=True
    ).astype(jnp.float32)
    hidden_part = (jax.nn.silu(owned[:, :unit_width]) * owned[:, unit_width:]).astype(jnp.bfloat16)
    hidden_all = lax.all_gather(hidden_part, ("red", "sub"), axis=0, tiled=True)
    return lax.psum_scatter(
        jnp.dot(hidden_all, down_kept, preferred_element_type=jnp.float32).astype(jnp.bfloat16),
        "blk",
        scatter_dimension=0,
        tiled=True,
    )


def solution(mesh):
    return jax.shard_map(
        per_device,
        mesh=mesh,
        in_specs=(
            P(("groups", "blk"), ("red", "sub")),
            P(("red", "sub"), "blk"),
            P(("red", "sub"), "blk"),
            P("blk", ("red", "sub")),
            P(("red", "sub"), "blk"),
            P("blk", ("red", "sub")),
        ),
        out_specs=P(("groups", "blk"), ("red", "sub")),
        check_vma=False,
    )
```

profile of v0, /device:TPU:0, one launch (start us, length us, event | category | flops | bytes accessed | tf_op | source)
XLA Modules:
  0.0 171.2 jit_solution(18111134438768056734)
XLA Ops:
  6.5 0.0 reduce-scatter.7.cloned.1.call-start
  6.5 0.7 broadcast_compare_fusion.1
  7.2 17.6 %all_gather.6 = bf16[128,2048]{1,0:T(8,128)(2,1)S(1)} all-gather(bf16[32,2048]{1,0:T(8,128)(2,1)} %param.6), channel_id=1, replica_groups=mesh['groups'=2,'blk'=4,'red'=2,'sub'=2] {'blk'}, dimensions={0}, use_global_device_ids=true | all-gather | bytes 655360 | tf_op jit(solution)/shard_map/all_gather | solution.py:22
  24.8 5.4 %broadcast_in_dim.29 = pred[16,128,32,128]{3,2,1,0:T(8,128)(4,1)} broadcast(pred[16,32]{1,0:T(8,128)(4,1)S(1)} %broadcast_compare_fusion.1), dimensions={0,2} | broadcast | bytes 8389120 | tf_op jit(solution)/shard_map/jit(_where)/broadcast_in_dim | solution.py:12
  30.2 25.4 %bitcast_select_fusion.2 = (bf16[2048,4096]{1,0:T(8,128)(2,1)}, bf16[2048,4096]{1,0:T(8,128)(2,1)}) fusion(bf16[2048,4096]{1,0:T(8,128)(2,1)} %param.7, pred[256,8,32,128]{3,2,1,0:T(8,128)(4,1)} %bitcast.17, bf16[2048,4096]{1,0:T(8,128)(2,1)} %param.8), kind=kLoop, calls=%fused_computation.6 | loop fusion | flops 16777216 | bytes 75497472 | tf_op jit(solution)/shard_map/jit(_where)/select_n | solution.py:12
  55.6 0.0 copy-start
  55.6 14.5 %fusion.8 = bf16[128,8192]{0,1:T(8,128)(2,1)S(1)} fusion(bf16[128,2048]{1,0:T(8,128)(2,1)S(1)} %all_gather.6, bf16[2048,4096]{1,0:T(8,128)(2,1)} %get-tuple-element.6, bf16[2048,4096]{1,0:T(8,128)(2,1)} %get-tuple-element.5), kind=kOutput, calls=%fused_computation.9 | convolution fusion | flops 4363124736 | bytes 36175872 | tf_op jit(solution)/shard_map/dot_general | solution.py:21
  70.1 3.0 %copy.12 = bf16[128,8192]{1,0:T(8,128)(2,1)} copy(bf16[128,8192]{0,1:T(8,128)(2,1)S(1)} %fusion.8) | data formatting | bytes 4194304
  73.0 0.0 reduce-scatter.7.cloned.1.call-update
  73.1 0.0 all-gather.2.cloned.1.call-start
  73.1 33.3 %reduce-scatter.7.cloned.1.call-done = bf16[32,8192]{1,0:T(8,128)(2,1)} async-done(((bf16[128,8192]{1,0:T(8,128)(2,1)}), bf16[32,8192]{1,0:T(8,128)(2,1)}) %reduce-scatter.7.cloned.1.call-update) | async-done | bytes 524304 | tf_op jit(solution)/shard_map/reduce_scatter | solution.py:26
  106.4 1.1 convert_element_type.17
  107.5 0.8 fusion.13
  108.4 0.0 all-gather.2.cloned.1.call-update
  108.4 0.0 reduce-scatter.5.cloned.1.call-start
  108.4 0.0 copy-done
  108.5 0.1 copy.11
  108.6 16.7 %all-gather.2.cloned.1.call-done = bf16[128,4096]{1,0:T(8,128)(2,1)} async-done(((bf16[32,4096]{1,0:T(8,128)(2,1)}), bf16[128,4096]{1,0:T(8,128)(2,1)}) %all-gather.2.cloned.1.call-update) | async-done | bytes 1048592 | tf_op jit(solution)/shard_map/all_gather | solution.py:30
  125.3 5.5 %broadcast_in_dim.31 = pred[32,128,16,128]{3,2,1,0:T(8,128)(4,1)} broadcast(pred[32,16]{1,0:T(8,128)(4,1)S(1)} %copy.11), dimensions={0,2} | broadcast | bytes 8389120 | tf_op jit(solution)/shard_map/jit(_where)/broadcast_in_dim | solution.py:12
  130.7 12.1 %fusion.12 = bf16[128,2048]{1,0:T(8,128)(2,1)} fusion(bf16[128,4096]{1,0:T(8,128)(2,1)} %all-gather.2.cloned.1.call-done, bf16[4096,2048]{1,0:T(8,128)(2,1)} %param.9, pred[512,8,16,128]{3,2,1,0:T(8,128)(4,1)} %bitcast.18), kind=kOutput, calls=%fused_computation.11 | convolution fusion | flops 2156134400 | bytes 26738688 | tf_op jit(solution)/shard_map/dot_general | solution.py:32
  142.8 0.0 reduce-scatter.5.cloned.1.call-update
  142.9 21.8 %reduce-scatter.5.cloned.1.call-done = bf16[32,2048]{1,0:T(8,128)(2,1)} async-done(((bf16[128,2048]{1,0:T(8,128)(2,1)}), bf16[32,2048]{1,0:T(8,128)(2,1)}) %reduce-scatter.5.cloned.1.call-update) | async-done | bytes 131088 | tf_op jit(solution)/shard_map/reduce_scatter | solution.py:31
  (1 shorter events, 0.0 us)
Async XLA Ops:
  6.5 99.9 %reduce-scatter.7.cloned.1.call-start = ((), (), s32[]{:S(2)}) async-start(), calls=%async_computation.4 | async-start | bytes 2621440 | tf_op jit(solution)/shard_map/reduce_scatter | solution.py:26
  55.6 52.9 %copy-start = (s32[32,16]{0,1:T(8,128)S(1)}, s32[32,16]{0,1:T(8,128)}, u32[]{:S(2)}) copy-start(s32[32,16]{0,1:T(8,128)} %param.11) | copy-start | bytes 6148
  73.1 52.2 %all-gather.2.cloned.1.call-start = ((), (), s32[]{:S(2)}) async-start(), calls=%async_computation.2 | async-start | bytes 1310720 | tf_op jit(solution)/shard_map/all_gather | solution.py:30
  108.4 56.3 %reduce-scatter.5.cloned.1.call-start = ((), (), s32[]{:S(2)}) async-start(), calls=%async_computation.3 | async-start | bytes 655360 | tf_op jit(solution)/shard_map/reduce_scatter | solution.py:31
Sparse Core Ops, SparseCore 0:
  73.2 33.1 reduce-scatter.6
  108.5 16.7 all-gather.1
  143.0 21.6 reduce-scatter.4
where the time goes:
time: 171 us
  waiting for transfers between devices  71.9 us (42%)
  other arithmetic  28 us (16%)
  matrix products  26.6 us (16%)
  blocking collectives  17.6 us (10%)
  local copies, waits for them, and re-layouts  14 us (8%)
  between operations  13.1 us (8%)
    reduce_scatter x1, waiting for transfers between devices, per_device(): lax.psum_scatter(partial_units.astype(jnp.bfloat16), ('red', 'sub'), scat...  33.3 us
    select_n x1, other arithmetic, expand_blocks(): jnp.where(kept_blocks, shaped, jnp.zeros_like(shaped))  25.4 us
    reduce_scatter x1, waiting for transfers between devices, per_device(): lax.psum_scatter(jnp.dot(hidden_all, down_kept, preferred_element_type=jn...  21.8 us
    all_gather x1, blocking collectives, per_device(): lax.all_gather(tokens, 'blk', axis=0, tiled=True)  17.6 us
    all_gather x1, waiting for transfers between devices, per_device(): hidden_all = lax.all_gather(hidden_part, ('red', 'sub'), axis=0, tiled=True)  16.7 us
    dot_general x1, matrix products, per_device(): jnp.dot(lax.all_gather(tokens, 'blk', axis=0, tiled=True), paired, prefer...  14.5 us
    dot_general x1, matrix products, per_device(): jnp.dot(hidden_all, down_kept, preferred_element_type=jnp.float32)  12.1 us
    broadcast_in_dim x2, local copies, waits for them, and re-layouts, expand_blocks(): jnp.where(kept_blocks, shaped, jnp.zeros_like(shaped))  10.9 us
  transfers between devices with their start and end apart: 3, of which 3 were waited for; matrix products, arithmetic and copies ran while one was open for 0% of the time, Pallas kernels for 0%

commit v1 on v0

--- a/solution.py
+++ b/solution.py
@@ -1,7 +1,19 @@
+import functools
+
 import jax
 import jax.numpy as jnp
 from jax import lax
+from jax.experimental import pallas as pl
+from jax.experimental.pallas import tpu as pltpu
 from jax.sharding import PartitionSpec as P
+
+BLOCK = 128
+CHUNKS = 4
+HALVES = 2
+VMEM_BYTES = 62 * 1024 * 1024
+MESH = pl.DeviceIdType.MESH
+F32 = jnp.float32
+BF16 = jnp.bfloat16
 
 
 def expand_blocks(weight, block_mask):
@@ -12,7 +24,7 @@
     return jnp.where(kept_blocks, shaped, jnp.zeros_like(shaped)).reshape(row_count, col_count)
 
 
-def per_device(tokens, gate_weight, up_weight, down_weight, in_mask, out_mask):
+def general_device(tokens, gate_weight, up_weight, down_weight, in_mask, out_mask):
     paired = jnp.concatenate(
         [expand_blocks(gate_weight, in_mask), expand_blocks(up_weight, in_mask)], axis=1
     )
@@ -36,7 +48,338 @@
     )
 
 
+def remote(src, dst, send, recv, where):
+    return pltpu.make_async_remote_copy(
+        src_ref=src, dst_ref=dst, send_sem=send, recv_sem=recv, device_id=where, device_id_type=MESH
+    )
+
+
+def iota(shape, dim):
+    return lax.broadcasted_iota(jnp.int32, shape, dim)
+
+
+def kernel(
+    n,
+    tokens, gate, up, down, in_mask, out_mask, out,
+    tok, gbuf, ubuf, dbuf, maskx, maskd, rows_in, cols_out,
+    asend, arecv, own, bsend, brecv, osum, hid, acc, term, zr,
+    tsem, gsem, usem, dsem, zsend, zrecv, a_s, a_r, b_s, b_r, cx_s, cx_r, cs_s, cs_r, cf_s, cf_r, o_s, o_r,
+):
+    chunks, owners, depth, width = gbuf.shape
+    halves, half = dbuf.shape[1], dbuf.shape[4]
+    share = chunks * width
+    z = lax.axis_index("blk")
+    r = lax.axis_index("red")
+    s = lax.axis_index("sub")
+    me = 2 * r + s
+    over_x = {"red": 1 - r}
+    over_core = {"sub": 1 - s}
+
+    local_tok = pltpu.make_async_copy(tokens, tok.at[z], tsem)
+    local_tok.start()
+
+    def cols_of(c, q):
+        return pl.ds(pl.multiple_of(q * share + c * width, width), width)
+
+    def load_in(c, q):
+        return (
+            pltpu.make_async_copy(gate.at[:, cols_of(c, q)], gbuf.at[c, q], gsem.at[c, q]),
+            pltpu.make_async_copy(up.at[:, cols_of(c, q)], ubuf.at[c, q], usem.at[c, q]),
+        )
+
+    def load_down(c, h, q):
+        return pltpu.make_async_copy(
+            down.at[cols_of(c, q), pl.ds(pl.multiple_of(h * half, half), half)],
+            dbuf.at[c, h, q],
+            dsem.at[c, h, q],
+        )
+
+    @pl.loop(0, chunks * owners)
+    def _(i):
+        for copy in load_in(i // owners, i % owners):
+            copy.start()
+
+    barrier = pltpu.get_barrier_semaphore()
+    for d in range(1, n):
+        pl.semaphore_signal(barrier, inc=1, device_id={"blk": lax.rem(z + d, n)}, device_id_type=MESH)
+    pl.semaphore_signal(barrier, inc=1, device_id=over_x, device_id_type=MESH)
+    pl.semaphore_signal(barrier, inc=1, device_id=over_core, device_id_type=MESH)
+    pl.semaphore_wait(barrier, n + 1)
+    local_tok.wait()
+
+    def hop_up(k):
+        shard = jnp.maximum(z - k, 0)
+        return remote(tok.at[shard], tok.at[shard], zsend.at[0, k], zrecv.at[0, k], {"blk": jnp.minimum(z + 1, n - 1)})
+
+    def hop_down(k):
+        shard = jnp.minimum(z + k, n - 1)
+        return remote(tok.at[shard], tok.at[shard], zsend.at[1, k], zrecv.at[1, k], {"blk": jnp.maximum(z - 1, 0)})
+
+    def start_hops(k):
+        @pl.when(jnp.logical_and(z >= k, z < n - 1))
+        def _():
+            hop_up(k).start()
+
+        @pl.when(jnp.logical_and(z + k <= n - 1, z > 0))
+        def _():
+            hop_down(k).start()
+
+    def wait_hops(k):
+        @pl.when(z >= k + 1)
+        def _():
+            shard = jnp.maximum(z - 1 - k, 0)
+            remote(tok.at[shard], tok.at[shard], zsend.at[0, k], zrecv.at[0, k], {"blk": jnp.minimum(z + 1, n - 1)}).wait_recv()
+
+        @pl.when(z + 1 + k <= n - 1)
+        def _():
+            shard = jnp.minimum(z + 1 + k, n - 1)
+            remote(tok.at[shard], tok.at[shard], zsend.at[1, k], zrecv.at[1, k], {"blk": jnp.maximum(z - 1, 0)}).wait_recv()
+
+    start_hops(0)
+
+    @pl.loop(0, chunks * halves * owners)
+    def _(i):
+        load_down(i // (halves * owners), (i // owners) % halves, i % owners).start()
+
+    blocks_in, blocks_unit = in_mask.shape
+    blocks_out = out_mask.shape[1]
+    kept_in = (in_mask[...] == 1).astype(F32).astype(BF16)
+    kept_out = (out_mask[...] == 1).astype(F32).astype(BF16)
+    repeat = (iota((blocks_in * 16, blocks_in), 0) // 16 == iota((blocks_in * 16, blocks_in), 1)).astype(F32).astype(BF16)
+    rows_in[...] = jnp.dot(repeat, kept_in, preferred_element_type=F32).astype(BF16)
+    spread = (iota((blocks_out, halves * half), 1) // BLOCK == iota((blocks_out, halves * half), 0)).astype(F32).astype(BF16)
+    cols_out[...] = jnp.dot(kept_out, spread, preferred_element_type=F32).astype(BF16)
+
+    for k in range(n - 1):
+        wait_hops(k)
+        if k < n - 2:
+            start_hops(k + 1)
+
+    def partial_sum(c, q):
+        for copy in load_in(c, q):
+            copy.wait()
+        first = (q * share + c * width) // BLOCK
+        pick = (iota((blocks_unit, width), 1) // BLOCK + first == iota((blocks_unit, width), 0)).astype(F32).astype(BF16)
+        kept = jnp.dot(rows_in[...], pick, preferred_element_type=F32).astype(BF16)
+        kept = jnp.broadcast_to(
+            kept.reshape(blocks_in, 1, 16, width), (blocks_in, BLOCK // 16, 16, width)
+        ).reshape(depth, width)
+        left = tok[...].reshape(-1, depth)
+        return (
+            jnp.dot(left, gbuf[c, q] * kept, preferred_element_type=F32),
+            jnp.dot(left, ubuf[c, q] * kept, preferred_element_type=F32),
+        )
+
+    def send_a(c):
+        return remote(asend.at[c], arecv.at[c], a_s.at[c], a_r.at[c], over_core)
+
+    def send_b(c):
+        return remote(bsend.at[c], brecv.at[c], b_s.at[c], b_r.at[c], over_x)
+
+    def send_cx(c, q):
+        return remote(hid.at[c, q], hid.at[c, q], cx_s.at[c], cx_r.at[c], over_x)
+
+    def send_cs(c, q):
+        return remote(hid.at[c, q], hid.at[c, q], cs_s.at[c], cs_r.at[c], over_core)
+
+    def send_cf(c, q):
+        return remote(hid.at[c, q], hid.at[c, q], cf_s.at[c], cf_r.at[c], over_core)
+
+    across = 2 * (1 - r) + s
+    beside = 2 * r + (1 - s)
+    far = 2 * (1 - r) + (1 - s)
+
+    def out_copy(h, d):
+        to = lax.rem(z + d, n)
+        return remote(term.at[h, to], zr.at[h, d - 1], o_s.at[h, d - 1], o_r.at[h, d - 1], {"blk": to})
+
+    def down_chunk(c):
+        for q in range(owners):
+            first = (q * share + c * width) // BLOCK
+            count = width // BLOCK * 16
+            pick = (iota((count, blocks_unit), 0) // 16 + first == iota((count, blocks_unit), 1)).astype(F32).astype(BF16)
+            maskd[q] = jnp.dot(pick, cols_out[...], preferred_element_type=F32).astype(BF16)
+        left = jnp.concatenate([hid[c, q] for q in range(owners)], axis=1)
+        for h in range(halves):
+            @pl.loop(0, owners)
+            def _(q):
+                load_down(c, h, q).wait()
+
+            kept = maskd[:, :, h * half : (h + 1) * half]
+            kept = jnp.broadcast_to(
+                kept.reshape(owners * (width // BLOCK), 1, 16, half),
+                (owners * (width // BLOCK), BLOCK // 16, 16, half),
+            ).reshape(owners * width, half)
+            value = jnp.dot(left, dbuf[c, h].reshape(owners * width, half) * kept, preferred_element_type=F32)
+
+            @pl.when(c == 0)
+            def _():
+                acc[h] = value
+
+            @pl.when(c > 0)
+            def _():
+                acc[h] += value
+
+            @pl.when(c == chunks - 1)
+            def _():
+                term[h] = acc[h].reshape(n, -1, half).astype(BF16)
+                for d in range(1, n):
+                    out_copy(h, d).start()
+
+    @pl.loop(0, chunks + 3)
+    def _(t):
+        @pl.when(t < chunks)
+        def _():
+            c = t
+
+            @pl.loop(0, 2)
+            def _(j):
+                g, u = partial_sum(c, 2 * j + (1 - s))
+                asend[c, j, :, :width] = g.astype(BF16)
+                asend[c, j, :, width:] = u.astype(BF16)
+
+            send_a(c).start()
+
+            @pl.loop(0, 2)
+            def _(j):
+                g, u = partial_sum(c, 2 * j + s)
+                own[j, :, :width] = g
+                own[j, :, width:] = u
+
+            send_a(c).wait_recv()
+            bsend[c] = (own[1 - r] + arecv[c, 1 - r].astype(F32)).astype(BF16)
+            send_b(c).start()
+            osum[t % 2] = own[r] + arecv[c, r].astype(F32)
+
+        @pl.when(jnp.logical_and(t >= 1, t <= chunks))
+        def _():
+            c = t - 1
+            send_b(c).wait_recv()
+            total = osum[c % 2] + brecv[c].astype(F32)
+            g, u = total[:, :width], total[:, width:]
+            hid[c, me] = (g / (1.0 + jnp.exp(-g)) * u).astype(BF16)
+            send_cx(c, me).start()
+            send_cs(c, me).start()
+
+        @pl.when(jnp.logical_and(t >= 2, t <= chunks + 1))
+        def _():
+            c = t - 2
+            send_cx(c, across).wait_recv()
+            send_cf(c, across).start()
+
+        @pl.when(t >= 3)
+        def _():
+            c = t - 3
+            send_cs(c, beside).wait_recv()
+            send_cf(c, far).wait_recv()
+            down_chunk(c)
+
+    for h in range(halves):
+        total = acc[h].reshape(n, -1, half)
+        mine = jnp.zeros(total.shape[1:], F32)
+        for j in range(n):
+            mine = mine + jnp.where(z == j, total[j], 0.0)
+        for d in range(1, n):
+            out_copy(h, d).wait_recv()
+            mine = mine + zr[h, d - 1].astype(F32)
+        out[:, h * half : (h + 1) * half] = mine.astype(BF16)
+
+    for k in range(n - 1):
+        @pl.when(jnp.logical_and(z >= k, z < n - 1))
+        def _():
+            hop_up(k).wait_send()
+
+        @pl.when(jnp.logical_and(z + k <= n - 1, z > 0))
+        def _():
+            hop_down(k).wait_send()
+
+    @pl.loop(0, chunks)
+    def _(c):
+        send_a(c).wait_send()
+        send_b(c).wait_send()
+        send_cx(c, me).wait_send()
+        send_cs(c, me).wait_send()
+        send_cf(c, across).wait_send()
+
+    for h in range(halves):
+        for d in range(1, n):
+            out_copy(h, d).wait_send()
+
+
+def fused_device(n, tokens, gate_weight, up_weight, down_weight, in_mask, out_mask):
+    rows, depth = tokens.shape
+    units = gate_weight.shape[1]
+    cols = down_weight.shape[1]
+    owners, chunks, halves = 4, CHUNKS, HALVES
+    width = units // (owners * chunks)
+    half = cols // halves
+    total = n * rows
+    dma = pltpu.SemaphoreType.DMA
+    vmem = pltpu.VMEM
+    anywhere = pl.BlockSpec(memory_space=pl.ANY)
+    in_vmem = pl.BlockSpec(memory_space=pltpu.VMEM)
+    return pl.pallas_call(
+        functools.partial(kernel, n),
+        out_shape=jax.ShapeDtypeStruct((rows, cols), BF16),
+        in_specs=[anywhere] * 4 + [in_vmem] * 2,
+        out_specs=in_vmem,
+        scratch_shapes=[
+            vmem((n, rows, depth), BF16),
+            vmem((chunks, owners, depth, width), BF16),
+            vmem((chunks, owners, depth, width), BF16),
+            vmem((chunks, halves, owners, width, half), BF16),
+            vmem((16, 128), BF16),
+            vmem((owners, width // BLOCK * 16, cols), BF16),
+            vmem((in_mask.shape[0] * 16, in_mask.shape[1]), BF16),
+            vmem((out_mask.shape[0], cols), BF16),
+            vmem((chunks, 2, total, 2 * width), BF16),
+            vmem((chunks, 2, total, 2 * width), BF16),
+            vmem((2, total, 2 * width), F32),
+            vmem((chunks, total, 2 * width), BF16),
+            vmem((chunks, total, 2 * width), BF16),
+            vmem((2, total, 2 * width), F32),
+            vmem((chunks, owners, total, width), BF16),
+            vmem((halves, total, half), F32),
+            vmem((halves, n, rows, half), BF16),
+            vmem((halves, n - 1, rows, half), BF16),
+            dma(()),
+            dma((chunks, owners)),
+            dma((chunks, owners)),
+            dma((chunks, halves, owners)),
+            dma((2, n - 1)),
+            dma((2, n - 1)),
+        ]
+        + [dma((chunks,))] * 10
+        + [dma((halves, n - 1))] * 2,
+        compiler_params=pltpu.CompilerParams(
+            collective_id=0, has_side_effects=True, vmem_limit_bytes=VMEM_BYTES
+        ),
+        cost_estimate=pl.CostEstimate(
+            flops=2 * total * (2 * depth * units + units * cols),
+            bytes_accessed=2 * (2 * depth * units + units * cols),
+            transcendentals=0,
+        ),
+    )(tokens, gate_weight, up_weight, down_weight, in_mask, out_mask)
+
+
 def solution(mesh):
+    n = mesh.shape["blk"]
+
+    def per_device(tokens, gate_weight, up_weight, down_weight, in_mask, out_mask):
+        weight_bytes = 2 * (gate_weight.size + up_weight.size + down_weight.size)
+        fits = (
+            mesh.shape["red"] == 2
+            and mesh.shape["sub"] == 2
+            and 2 <= n <= 4
+            and weight_bytes <= 48 * 1024 * 1024
+            and tokens.shape[0] % 16 == 0
+            and n * tokens.shape[0] <= 128
+            and gate_weight.shape[1] % (4 * CHUNKS * 256) == 0
+            and down_weight.shape[1] % (HALVES * 256) == 0
+        )
+        args = (tokens, gate_weight, up_weight, down_weight, in_mask, out_mask)
+        return fused_device(n, *args) if fits else general_device(*args)
+
     return jax.shard_map(
         per_device,
         mesh=mesh,

time: 171 us -> 58 us (0.34)
  waiting for transfers between devices: 71.9 us -> 0 us
  Pallas kernels: 0 us -> 54.7 us
  other arithmetic: 28 us -> 0 us
  matrix products: 26.6 us -> 0 us
  blocking collectives: 17.6 us -> 0 us
  between operations: 13.1 us -> 0.01 us
  local copies, waits for them, and re-layouts: 14 us -> 2.94 us
    reduce_scatter x2 -> x0, waiting for transfers between devices: 55.1 us -> none  [the longest x1 33.3 us: per_device(): lax.psum_scatter(partial_units.astype(jnp.bfloat16), ('red', 'sub'), scat...]
    pallas_call x0 -> x1, Pallas kernels: none -> 54.7 us  [fused_device(): pl.pallas_call(functools.partial(kernel, n), out_shape=jax.ShapeDtypeStru...]
    dot_general x2 -> x0, matrix products: 26.6 us -> none  [the longest x1 14.5 us: per_device(): jnp.dot(lax.all_gather(tokens, 'blk', axis=0, tiled=True), paired, prefer...]
    select_n x1 -> x0, other arithmetic: 25.4 us -> none  [expand_blocks(): jnp.where(kept_blocks, shaped, jnp.zeros_like(shaped))]
    all_gather x1 -> x0, blocking collectives: 17.6 us -> none  [per_device(): lax.all_gather(tokens, 'blk', axis=0, tiled=True)]
    all_gather x1 -> x0, waiting for transfers between devices: 16.7 us -> none  [per_device(): hidden_all = lax.all_gather(hidden_part, ('red', 'sub'), axis=0, tiled=True)]
    broadcast_in_dim x2 -> x0, local copies, waits for them, and re-layouts: 10.9 us -> none  [expand_blocks(): jnp.where(kept_blocks, shaped, jnp.zeros_like(shaped))]
    convert_element_type x2 -> x0, other arithmetic: 1.96 us -> none  [the longest x1 1.11 us: per_device(): owned = lax.psum_scatter(partial_units.astype(jnp.bfloat16), ('red', 'sub...]
  transfers between devices with their start and end apart: 3 -> 0, of which waited for: 3 -> 0; matrix products, arithmetic and copies ran while one was open for 0% -> 0% of each run, Pallas kernels for 0% -> 0%
where the time goes in v1:
time: 58 us; the launch traced here: 57.6 us
  Pallas kernels  54.7 us (94%)
  local copies, waits for them, and re-layouts  2.94 us (5%)
    pallas_call x1, Pallas kernels, fused_device(): pl.pallas_call(functools.partial(kernel, n), out_shape=jax.ShapeDtypeStru...  54.7 us
    unnamed x2, local copies, waits for them, and re-layouts  2.94 us

profile of v1, /device:TPU:0, one launch (start us, length us, event | category | flops | bytes accessed | tf_op | source)
XLA Modules:
  0.0 57.6 jit_solution(15698240389611370328)
XLA Ops:
  0.0 1.4 %copy.7.out_mask = s32[32,16]{1,0:T(8,128)} copy(s32[32,16]{0,1:T(8,128)} %param.11) | data formatting | bytes 4096 | tf_op args[5]
  1.4 54.7 %shard_map.64 = bf16[32,2048]{1,0:T(8,128)(2,1)} custom-call(bf16[32,2048]{1,0:T(8,128)(2,1)} %tokens.1, bf16[2048,4096]{1,0:T(8,128)(2,1)} %gate.1, bf16[2048,4096]{1,0:T(8,128)(2,1)} %up.1, bf16[4096,2048]{1,0:T(8,128)(2,1)} %down.1, s32[16,32]{1,0:T(8,128)} %in_mask.1, s32[32,16]{1,0:T(8,128)} %copy.7.out_mask), custom_call_target="tpu_custom_call" | custom-call | flops 6442450944 | bytes 50331648 | tf_op jit(solution)/shard_map/pallas_call | solution.py:321
  56.1 1.6 %copy.9 = bf16[32,2048]{1,0:T(8,128)(2,1)} copy(bf16[32,2048]{1,0:T(8,128)(2,1)} %shard_map.64) | data formatting | bytes 262144

commit v2 on v1

--- a/solution.py
+++ b/solution.py
@@ -10,6 +10,7 @@
 BLOCK = 128
 CHUNKS = 4
 HALVES = 2
+PIECES = 2
 VMEM_BYTES = 62 * 1024 * 1024
 MESH = pl.DeviceIdType.MESH
 F32 = jnp.float32
@@ -62,8 +63,8 @@
     n,
     tokens, gate, up, down, in_mask, out_mask, out,
     tok, gbuf, ubuf, dbuf, maskx, maskd, rows_in, cols_out,
-    asend, arecv, own, bsend, brecv, osum, hid, acc, term, zr,
-    tsem, gsem, usem, dsem, zsend, zrecv, a_s, a_r, b_s, b_r, cx_s, cx_r, cs_s, cs_r, cf_s, cf_r, o_s, o_r,
+    asend, arecv, own, bsend, brecv, osum, hid, acc, term, zr, zin,
+    tsem, gsem, usem, dsem, zsend, zrecv, a_s, a_r, b_s, b_r, cx_s, cx_r, cs_s, cs_r, cf_s, cf_r, o_s, o_r, m_s, m_r,
 ):
     chunks, owners, depth, width = gbuf.shape
     halves, half = dbuf.shape[1], dbuf.shape[4]
@@ -107,53 +108,49 @@
     pl.semaphore_wait(barrier, n + 1)
     local_tok.wait()
 
-    def hop_up(k):
-        shard = jnp.maximum(z - k, 0)
-        return remote(tok.at[shard], tok.at[shard], zsend.at[0, k], zrecv.at[0, k], {"blk": jnp.minimum(z + 1, n - 1)})
-
-    def hop_down(k):
-        shard = jnp.minimum(z + k, n - 1)
-        return remote(tok.at[shard], tok.at[shard], zsend.at[1, k], zrecv.at[1, k], {"blk": jnp.maximum(z - 1, 0)})
-
-    def start_hops(k):
-        @pl.when(jnp.logical_and(z >= k, z < n - 1))
-        def _():
-            hop_up(k).start()
-
-        @pl.when(jnp.logical_and(z + k <= n - 1, z > 0))
-        def _():
-            hop_down(k).start()
-
-    def wait_hops(k):
-        @pl.when(z >= k + 1)
-        def _():
-            shard = jnp.maximum(z - 1 - k, 0)
-            remote(tok.at[shard], tok.at[shard], zsend.at[0, k], zrecv.at[0, k], {"blk": jnp.minimum(z + 1, n - 1)}).wait_recv()
-
-        @pl.when(z + 1 + k <= n - 1)
-        def _():
-            shard = jnp.minimum(z + 1 + k, n - 1)
-            remote(tok.at[shard], tok.at[shard], zsend.at[1, k], zrecv.at[1, k], {"blk": jnp.maximum(z - 1, 0)}).wait_recv()
-
-    start_hops(0)
+    rows = tok.shape[1] // PIECES
+
+    def hop(way, k, p, shard):
+        shard = jnp.clip(shard, 0, n - 1)
+        part = tok.at[shard, pl.ds(p * rows, rows)]
+        to = jnp.clip(z + (1 if way == 0 else -1), 0, n - 1)
+        return remote(part, part, zsend.at[way, k, p], zrecv.at[way, k, p], {"blk": to})
+
+    def start_hops(way, k, p):
+        @pl.when(jnp.logical_and(z >= k, z < n - 1) if way == 0 else jnp.logical_and(z + k <= n - 1, z > 0))
+        def _():
+            hop(way, k, p, z - k if way == 0 else z + k).start()
+
+    def wait_hops(way, k, p):
+        @pl.when(z >= k + 1 if way == 0 else z + 1 + k <= n - 1)
+        def _():
+            hop(way, k, p, z - 1 - k if way == 0 else z + 1 + k).wait_recv()
+
+    for p in range(PIECES):
+        for way in range(2):
+            start_hops(way, 0, p)
 
     @pl.loop(0, chunks * halves * owners)
     def _(i):
         load_down(i // (halves * owners), (i // owners) % halves, i % owners).start()
 
     blocks_in, blocks_unit = in_mask.shape
-    blocks_out = out_mask.shape[1]
+    blocks_out = out_mask.shape[0]
     kept_in = (in_mask[...] == 1).astype(F32).astype(BF16)
     kept_out = (out_mask[...] == 1).astype(F32).astype(BF16)
     repeat = (iota((blocks_in * 16, blocks_in), 0) // 16 == iota((blocks_in * 16, blocks_in), 1)).astype(F32).astype(BF16)
     rows_in[...] = jnp.dot(repeat, kept_in, preferred_element_type=F32).astype(BF16)
     spread = (iota((blocks_out, halves * half), 1) // BLOCK == iota((blocks_out, halves * half), 0)).astype(F32).astype(BF16)
-    cols_out[...] = jnp.dot(kept_out, spread, preferred_element_type=F32).astype(BF16)
+    cols_out[...] = lax.dot_general(
+        kept_out, spread, (((0,), (0,)), ((), ())), preferred_element_type=F32
+    ).astype(BF16)
 
     for k in range(n - 1):
-        wait_hops(k)
-        if k < n - 2:
-            start_hops(k + 1)
+        for p in range(PIECES):
+            for way in range(2):
+                wait_hops(way, k, p)
+                if k < n - 2:
+                    start_hops(way, k + 1, p)
 
     def partial_sum(c, q):
         for copy in load_in(c, q):
@@ -170,8 +167,8 @@
             jnp.dot(left, ubuf[c, q] * kept, preferred_element_type=F32),
         )
 
-    def send_a(c):
-        return remote(asend.at[c], arecv.at[c], a_s.at[c], a_r.at[c], over_core)
+    def send_a(c, j):
+        return remote(asend.at[c, j], arecv.at[c, j], a_s.at[c, j], a_r.at[c, j], over_core)
 
     def send_b(c):
         return remote(bsend.at[c], brecv.at[c], b_s.at[c], b_r.at[c], over_x)
@@ -189,9 +186,21 @@
     beside = 2 * r + (1 - s)
     far = 2 * (1 - r) + (1 - s)
 
-    def out_copy(h, d):
-        to = lax.rem(z + d, n)
-        return remote(term.at[h, to], zr.at[h, d - 1], o_s.at[h, d - 1], o_r.at[h, d - 1], {"blk": to})
+    outer = jnp.logical_or(z == 0, z == n - 1)
+    mate = jnp.where(z // 2 == 0, 1 - z, 5 - z)
+    far_end = jnp.where(z // 2 == 0, n - 1, 0)
+    far_mid = jnp.where(z // 2 == 0, 2, 1)
+
+    def to_mate(h):
+        return remote(term.at[h, mate], zr.at[h, 0], o_s.at[h, 0], o_r.at[h, 0], {"blk": mate})
+
+    def from_end(h, i):
+        src = term.at[h, far_end if i == 0 else far_mid]
+        return remote(src, zin.at[h, i], m_s.at[h, i], m_r.at[h, i], {"blk": mate})
+
+    def to_far(h, i):
+        to = far_end if i == 0 else far_mid
+        return remote(term.at[h, to], zr.at[h, 1], o_s.at[h, 1 + i], o_r.at[h, 1], {"blk": to})
 
     def down_chunk(c):
         for q in range(owners):
@@ -212,19 +221,28 @@
             ).reshape(owners * width, half)
             value = jnp.dot(left, dbuf[c, h].reshape(owners * width, half) * kept, preferred_element_type=F32)
 
+            value = value.reshape(n, -1, half)
+
             @pl.when(c == 0)
             def _():
                 acc[h] = value
 
-            @pl.when(c > 0)
+            @pl.when(jnp.logical_and(c > 0, c < chunks - 1))
             def _():
                 acc[h] += value
 
             @pl.when(c == chunks - 1)
             def _():
-                term[h] = acc[h].reshape(n, -1, half).astype(BF16)
-                for d in range(1, n):
-                    out_copy(h, d).start()
+                total = acc[h] + value
+                acc[h] = total
+                term[h] = total.astype(BF16)
+
+                @pl.when(outer)
+                def _():
+                    from_end(h, 0).start()
+                    from_end(h, 1).start()
+
+                to_mate(h).start()
 
     @pl.loop(0, chunks + 3)
     def _(t):
@@ -234,22 +252,25 @@
 
             @pl.loop(0, 2)
             def _(j):
-                g, u = partial_sum(c, 2 * j + (1 - s))
+                row = jnp.where(j == 0, 1 - r, r)
+                g, u = partial_sum(c, 2 * row + (1 - s))
                 asend[c, j, :, :width] = g.astype(BF16)
                 asend[c, j, :, width:] = u.astype(BF16)
-
-            send_a(c).start()
-
-            @pl.loop(0, 2)
-            def _(j):
-                g, u = partial_sum(c, 2 * j + s)
-                own[j, :, :width] = g
-                own[j, :, width:] = u
-
-            send_a(c).wait_recv()
-            bsend[c] = (own[1 - r] + arecv[c, 1 - r].astype(F32)).astype(BF16)
-            send_b(c).start()
-            osum[t % 2] = own[r] + arecv[c, r].astype(F32)
+                send_a(c, j).start()
+                g, u = partial_sum(c, 2 * row + s)
+                own[:, :width] = g
+                own[:, width:] = u
+                send_a(c, j).wait_recv()
+                summed = own[...] + arecv[c, j].astype(F32)
+
+                @pl.when(j == 0)
+                def _():
+                    bsend[c] = summed.astype(BF16)
+                    send_b(c).start()
+
+                @pl.when(j == 1)
+                def _():
+                    osum[c % 2] = summed
 
         @pl.when(jnp.logical_and(t >= 1, t <= chunks))
         def _():
@@ -274,36 +295,52 @@
             send_cf(c, far).wait_recv()
             down_chunk(c)
 
+    @pl.when(jnp.logical_not(outer))
+    def _():
+        for h in range(halves):
+            for i in range(2):
+                to = far_end if i == 0 else far_mid
+                from_end(h, i).wait_recv()
+                term[h, to] = (acc[h, to] + zin[h, i].astype(F32)).astype(BF16)
+                to_far(h, i).start()
+
     for h in range(halves):
-        total = acc[h].reshape(n, -1, half)
-        mine = jnp.zeros(total.shape[1:], F32)
-        for j in range(n):
-            mine = mine + jnp.where(z == j, total[j], 0.0)
-        for d in range(1, n):
-            out_copy(h, d).wait_recv()
-            mine = mine + zr[h, d - 1].astype(F32)
-        out[:, h * half : (h + 1) * half] = mine.astype(BF16)
+        to_mate(h).wait_recv()
+        mine = acc[h, z] + zr[h, 0].astype(F32)
+        to_far(h, 0).wait_recv()
+        out[:, h * half : (h + 1) * half] = (mine + zr[h, 1].astype(F32)).astype(BF16)
 
     for k in range(n - 1):
-        @pl.when(jnp.logical_and(z >= k, z < n - 1))
-        def _():
-            hop_up(k).wait_send()
-
-        @pl.when(jnp.logical_and(z + k <= n - 1, z > 0))
-        def _():
-            hop_down(k).wait_send()
+        for p in range(PIECES):
+            @pl.when(jnp.logical_and(z >= k, z < n - 1))
+            def _():
+                hop(0, k, p, z - k).wait_send()
+
+            @pl.when(jnp.logical_and(z + k <= n - 1, z > 0))
+            def _():
+                hop(1, k, p, z + k).wait_send()
 
     @pl.loop(0, chunks)
     def _(c):
-        send_a(c).wait_send()
+        send_a(c, 0).wait_send()
+        send_a(c, 1).wait_send()
         send_b(c).wait_send()
         send_cx(c, me).wait_send()
         send_cs(c, me).wait_send()
         send_cf(c, across).wait_send()
 
     for h in range(halves):
-        for d in range(1, n):
-            out_copy(h, d).wait_send()
+        to_mate(h).wait_send()
+
+        @pl.when(outer)
+        def _():
+            from_end(h, 0).wait_send()
+            from_end(h, 1).wait_send()
+
+        @pl.when(jnp.logical_not(outer))
+        def _():
+            to_far(h, 0).wait_send()
+            to_far(h, 1).wait_send()
 
 
 def fused_device(n, tokens, gate_weight, up_weight, down_weight, in_mask, out_mask):
@@ -334,23 +371,26 @@
             vmem((out_mask.shape[0], cols), BF16),
             vmem((chunks, 2, total, 2 * width), BF16),
             vmem((chunks, 2, total, 2 * width), BF16),
-            vmem((2, total, 2 * width), F32),
+            vmem((total, 2 * width), F32),
             vmem((chunks, total, 2 * width), BF16),
             vmem((chunks, total, 2 * width), BF16),
             vmem((2, total, 2 * width), F32),
             vmem((chunks, owners, total, width), BF16),
-            vmem((halves, total, half), F32),
+            vmem((halves, n, rows, half), F32),
             vmem((halves, n, rows, half), BF16),
-            vmem((halves, n - 1, rows, half), BF16),
+            vmem((halves, 2, rows, half), BF16),
+            vmem((halves, 2, rows, half), BF16),
             dma(()),
             dma((chunks, owners)),
             dma((chunks, owners)),
             dma((chunks, halves, owners)),
-            dma((2, n - 1)),
-            dma((2, n - 1)),
+            dma((2, n - 1, PIECES)),
+            dma((2, n - 1, PIECES)),
         ]
-        + [dma((chunks,))] * 10
-        + [dma((halves, n - 1))] * 2,
+        + [dma((chunks, 2))] * 2
+        + [dma((chunks,))] * 8
+        + [dma((halves, 3))] * 2
+        + [dma((halves, 2))] * 2,
         compiler_params=pltpu.CompilerParams(
             collective_id=0, has_side_effects=True, vmem_limit_bytes=VMEM_BYTES
         ),
@@ -359,7 +399,7 @@
             bytes_accessed=2 * (2 * depth * units + units * cols),
             transcendentals=0,
         ),
-    )(tokens, gate_weight, up_weight, down_weight, in_mask, out_mask)
+    )(tokens, gate_weight, up_weight, down_weight, in_mask, out_mask.T)
 
 
 def solution(mesh):
@@ -370,9 +410,9 @@
         fits = (
             mesh.shape["red"] == 2
             and mesh.shape["sub"] == 2
-            and 2 <= n <= 4
+            and n == 4
             and weight_bytes <= 48 * 1024 * 1024
-            and tokens.shape[0] % 16 == 0
+            and tokens.shape[0] % (16 * PIECES) == 0
             and n * tokens.shape[0] <= 128
             and gate_weight.shape[1] % (4 * CHUNKS * 256) == 0
             and down_weight.shape[1] % (HALVES * 256) == 0

time: 58 us -> 56.8 us (0.979)
  local copies, waits for them, and re-layouts: 2.94 us -> 1.57 us
    unnamed x2 -> x1, local copies, waits for them, and re-layouts: 2.94 us -> 1.57 us
where the time goes in v2:
time: 56.8 us; the launch traced here: 56.6 us
  Pallas kernels  55 us (97%)
  local copies, waits for them, and re-layouts  1.57 us (3%)
    pallas_call x1, Pallas kernels, fused_device(): pl.pallas_call(functools.partial(kernel, n), out_shape=jax.ShapeDtypeStru...  55 us
    unnamed x1, local copies, waits for them, and re-layouts  1.57 us

profile of v2, /device:TPU:0, one launch (start us, length us, event | category | flops | bytes accessed | tf_op | source)
XLA Modules:
  0.0 56.6 jit_solution(8387958225265041971)
XLA Ops:
  0.0 55.0 %shard_map.64 = bf16[32,2048]{1,0:T(8,128)(2,1)} custom-call(bf16[32,2048]{1,0:T(8,128)(2,1)} %tokens.1, bf16[2048,4096]{1,0:T(8,128)(2,1)} %gate.1, bf16[2048,4096]{1,0:T(8,128)(2,1)} %up.1, bf16[4096,2048]{1,0:T(8,128)(2,1)} %down.1, s32[16,32]{1,0:T(8,128)} %in_mask.1, s32[16,32]{1,0:T(8,128)} %bitcast.1), custom_call_target="tpu_custom_call" | custom-call | flops 6442450944 | bytes 50331648 | tf_op jit(solution)/shard_map/pallas_call | solution.py:358
  55.0 1.6 %copy.8 = bf16[32,2048]{1,0:T(8,128)(2,1)} copy(bf16[32,2048]{1,0:T(8,128)(2,1)} %shard_map.64) | data formatting | bytes 262144

commit v3 on v2

--- a/solution.py
+++ b/solution.py
@@ -11,6 +11,7 @@
 CHUNKS = 4
 HALVES = 2
 PIECES = 2
+EARLY = 2
 VMEM_BYTES = 62 * 1024 * 1024
 MESH = pl.DeviceIdType.MESH
 F32 = jnp.float32
@@ -145,42 +146,100 @@
         kept_out, spread, (((0,), (0,)), ((), ())), preferred_element_type=F32
     ).astype(BF16)
 
-    for k in range(n - 1):
+    def next_hops(k):
         for p in range(PIECES):
             for way in range(2):
                 wait_hops(way, k, p)
                 if k < n - 2:
                     start_hops(way, k + 1, p)
 
-    def partial_sum(c, q):
-        for copy in load_in(c, q):
-            copy.wait()
+    def partial_sum(c, q, part, slot):
+        if slot == 0:
+            for copy in load_in(c, q):
+                copy.wait()
         first = (q * share + c * width) // BLOCK
         pick = (iota((blocks_unit, width), 1) // BLOCK + first == iota((blocks_unit, width), 0)).astype(F32).astype(BF16)
         kept = jnp.dot(rows_in[...], pick, preferred_element_type=F32).astype(BF16)
         kept = jnp.broadcast_to(
             kept.reshape(blocks_in, 1, 16, width), (blocks_in, BLOCK // 16, 16, width)
         ).reshape(depth, width)
-        left = tok[...].reshape(-1, depth)
+        left = (tok[...] if part is None else tok[pl.ds(part * (n // 2), n // 2)]).reshape(-1, depth)
         return (
             jnp.dot(left, gbuf[c, q] * kept, preferred_element_type=F32),
             jnp.dot(left, ubuf[c, q] * kept, preferred_element_type=F32),
         )
 
-    def send_a(c, j):
-        return remote(asend.at[c, j], arecv.at[c, j], a_s.at[c, j], a_r.at[c, j], over_core)
-
-    def send_b(c):
-        return remote(bsend.at[c], brecv.at[c], b_s.at[c], b_r.at[c], over_x)
-
-    def send_cx(c, q):
-        return remote(hid.at[c, q], hid.at[c, q], cx_s.at[c], cx_r.at[c], over_x)
-
-    def send_cs(c, q):
-        return remote(hid.at[c, q], hid.at[c, q], cs_s.at[c], cs_r.at[c], over_core)
-
-    def send_cf(c, q):
-        return remote(hid.at[c, q], hid.at[c, q], cf_s.at[c], cf_r.at[c], over_core)
+    near = z // (n // 2)
+
+    def of(ref, part):
+        return ref if part is None else ref.at[part]
+
+    def send(src, dst, send_sem, recv_sem, part, where):
+        return remote(of(src, part), of(dst, part), send_sem, recv_sem, where)
+
+    def send_a(c, j, part, slot):
+        return send(asend.at[c, j], arecv.at[c, j], a_s.at[c, j, slot], a_r.at[c, j, slot], part, over_core)
+
+    def send_b(c, part, slot):
+        return send(bsend.at[c], brecv.at[c], b_s.at[c, slot], b_r.at[c, slot], part, over_x)
+
+    def send_cx(c, q, part, slot):
+        return send(hid.at[c, q], hid.at[c, q], cx_s.at[c, slot], cx_r.at[c, slot], part, over_x)
+
+    def send_cs(c, q, part, slot):
+        return send(hid.at[c, q], hid.at[c, q], cs_s.at[c, slot], cs_r.at[c, slot], part, over_core)
+
+    def send_cf(c, q, part, slot):
+        return send(hid.at[c, q], hid.at[c, q], cf_s.at[c, slot], cf_r.at[c, slot], part, over_core)
+
+    def unit(c, j, part, slot):
+        row = jnp.where(j == 0, 1 - r, r)
+        outgoing = of(asend.at[c, j], part)
+        mine = own if part is None else own.at[0]
+        shape = mine.shape[:-1] + (width,)
+        g, u = partial_sum(c, 2 * row + (1 - s), part, slot)
+        outgoing[..., :width] = g.astype(BF16).reshape(shape)
+        outgoing[..., width:] = u.astype(BF16).reshape(shape)
+        send_a(c, j, part, slot).start()
+        g, u = partial_sum(c, 2 * row + s, part, slot)
+        mine[..., :width] = g.reshape(shape)
+        mine[..., width:] = u.reshape(shape)
+        send_a(c, j, part, slot).wait_recv()
+        summed = mine[...] + of(arecv.at[c, j], part)[...].astype(F32)
+
+        @pl.when(j == 0)
+        def _():
+            of(bsend.at[c], part)[...] = summed.astype(BF16)
+            send_b(c, part, slot).start()
+
+        @pl.when(j == 1)
+        def _():
+            of(osum.at[c], part)[...] = summed
+
+    def activate(c, part, slot):
+        send_b(c, part, slot).wait_recv()
+        total = of(osum.at[c], part)[...] + of(brecv.at[c], part)[...].astype(F32)
+        g, u = total[..., :width], total[..., width:]
+        of(hid.at[c, me], part)[...] = (g / (1.0 + jnp.exp(-g)) * u).astype(BF16)
+        send_cx(c, me, part, slot).start()
+        send_cs(c, me, part, slot).start()
+
+    def hand_on(c, part, slot):
+        send_cx(c, across, part, slot).wait_recv()
+        send_cf(c, across, part, slot).start()
+
+    def gathered(c, part, slot):
+        send_cs(c, beside, part, slot).wait_recv()
+        send_cf(c, far, part, slot).wait_recv()
+
+    def split(c, step):
+        @pl.when(c < EARLY)
+        def _():
+            step(1 - near, 1)
+
+        @pl.when(c >= EARLY)
+        def _():
+            step(None, 0)
 
     across = 2 * (1 - r) + s
     beside = 2 * r + (1 - s)
@@ -208,7 +267,7 @@
             count = width // BLOCK * 16
             pick = (iota((count, blocks_unit), 0) // 16 + first == iota((count, blocks_unit), 1)).astype(F32).astype(BF16)
             maskd[q] = jnp.dot(pick, cols_out[...], preferred_element_type=F32).astype(BF16)
-        left = jnp.concatenate([hid[c, q] for q in range(owners)], axis=1)
+        left = jnp.concatenate([hid[c, q].reshape(-1, width) for q in range(owners)], axis=1)
         for h in range(halves):
             @pl.loop(0, owners)
             def _(q):
@@ -242,58 +301,66 @@
                     from_end(h, 0).start()
                     from_end(h, 1).start()
 
+        @pl.when(c == chunks - 1)
+        def _():
+            for h in range(halves):
                 to_mate(h).start()
+
+    next_hops(0)
+
+    @pl.loop(0, 2 * EARLY)
+    def _(i):
+        @pl.when(i == 1)
+        def _():
+            next_hops(1)
+
+        @pl.when(i == 2)
+        def _():
+            activate(0, near, 0)
+
+        @pl.when(i == 3)
+        def _():
+            next_hops(2)
+
+        unit(i // 2, i % 2, near, 0)
+
+    hand_on(0, near, 0)
+    activate(1, near, 0)
 
     @pl.loop(0, chunks + 3)
     def _(t):
-        @pl.when(t < chunks)
-        def _():
-            c = t
-
+        @pl.when(t < EARLY)
+        def _():
             @pl.loop(0, 2)
             def _(j):
-                row = jnp.where(j == 0, 1 - r, r)
-                g, u = partial_sum(c, 2 * row + (1 - s))
-                asend[c, j, :, :width] = g.astype(BF16)
-                asend[c, j, :, width:] = u.astype(BF16)
-                send_a(c, j).start()
-                g, u = partial_sum(c, 2 * row + s)
-                own[:, :width] = g
-                own[:, width:] = u
-                send_a(c, j).wait_recv()
-                summed = own[...] + arecv[c, j].astype(F32)
-
-                @pl.when(j == 0)
-                def _():
-                    bsend[c] = summed.astype(BF16)
-                    send_b(c).start()
-
-                @pl.when(j == 1)
-                def _():
-                    osum[c % 2] = summed
+                unit(t, j, 1 - near, 1)
+
+        @pl.when(jnp.logical_and(t >= EARLY, t < chunks))
+        def _():
+            @pl.loop(0, 2)
+            def _(j):
+                unit(t, j, None, 0)
+
+        @pl.when(t == 0)
+        def _():
+            hand_on(1, near, 0)
 
         @pl.when(jnp.logical_and(t >= 1, t <= chunks))
         def _():
-            c = t - 1
-            send_b(c).wait_recv()
-            total = osum[c % 2] + brecv[c].astype(F32)
-            g, u = total[:, :width], total[:, width:]
-            hid[c, me] = (g / (1.0 + jnp.exp(-g)) * u).astype(BF16)
-            send_cx(c, me).start()
-            send_cs(c, me).start()
+            split(t - 1, functools.partial(activate, t - 1))
 
         @pl.when(jnp.logical_and(t >= 2, t <= chunks + 1))
         def _():
-            c = t - 2
-            send_cx(c, across).wait_recv()
-            send_cf(c, across).start()
+            split(t - 2, functools.partial(hand_on, t - 2))
 
         @pl.when(t >= 3)
         def _():
-            c = t - 3
-            send_cs(c, beside).wait_recv()
-            send_cf(c, far).wait_recv()
-            down_chunk(c)
+            @pl.when(t - 3 < EARLY)
+            def _():
+                gathered(t - 3, near, 0)
+
+            split(t - 3, functools.partial(gathered, t - 3))
+            down_chunk(t - 3)
 
     @pl.when(jnp.logical_not(outer))
     def _():
@@ -320,14 +387,20 @@
             def _():
                 hop(1, k, p, z + k).wait_send()
 
-    @pl.loop(0, chunks)
-    def _(c):
-        send_a(c, 0).wait_send()
-        send_a(c, 1).wait_send()
-        send_b(c).wait_send()
-        send_cx(c, me).wait_send()
-        send_cs(c, me).wait_send()
-        send_cf(c, across).wait_send()
+    def sent(c, part, slot):
+        for j in range(2):
+            send_a(c, j, part, slot).wait_send()
+        send_b(c, part, slot).wait_send()
+        send_cx(c, me, part, slot).wait_send()
+        send_cs(c, me, part, slot).wait_send()
+        send_cf(c, across, part, slot).wait_send()
+
+    for c in range(chunks):
+        if c < EARLY:
+            sent(c, near, 0)
+            sent(c, 1 - near, 1)
+        else:
+            sent(c, None, 0)
 
     for h in range(halves):
         to_mate(h).wait_send()
@@ -369,13 +442,13 @@
             vmem((owners, width // BLOCK * 16, cols), BF16),
             vmem((in_mask.shape[0] * 16, in_mask.shape[1]), BF16),
             vmem((out_mask.shape[0], cols), BF16),
-            vmem((chunks, 2, total, 2 * width), BF16),
-            vmem((chunks, 2, total, 2 * width), BF16),
-            vmem((total, 2 * width), F32),
-            vmem((chunks, total, 2 * width), BF16),
-            vmem((chunks, total, 2 * width), BF16),
-            vmem((2, total, 2 * width), F32),
-            vmem((chunks, owners, total, width), BF16),
+            vmem((chunks, 2, 2, total // 2, 2 * width), BF16),
+            vmem((chunks, 2, 2, total // 2, 2 * width), BF16),
+            vmem((2, total // 2, 2 * width), F32),
+            vmem((chunks, 2, total // 2, 2 * width), BF16),
+            vmem((chunks, 2, total // 2, 2 * width), BF16),
+            vmem((chunks, 2, total // 2, 2 * width), F32),
+            vmem((chunks, owners, 2, total // 2, width), BF16),
             vmem((halves, n, rows, half), F32),
             vmem((halves, n, rows, half), BF16),
             vmem((halves, 2, rows, half), BF16),
@@ -387,8 +460,8 @@
             dma((2, n - 1, PIECES)),
             dma((2, n - 1, PIECES)),
         ]
-        + [dma((chunks, 2))] * 2
-        + [dma((chunks,))] * 8
+        + [dma((chunks, 2, 2))] * 2
+        + [dma((chunks, 2))] * 8
         + [dma((halves, 3))] * 2
         + [dma((halves, 2))] * 2,
         compiler_params=pltpu.CompilerParams(

time: 56.8 us -> 57.5 us (1.012)
  Pallas kernels: 55 us -> 55.7 us
    pallas_call x1, Pallas kernels: 55 us -> 55.7 us  [fused_device(): pl.pallas_call(functools.partial(kernel, n), out_shape=jax.ShapeDtypeStru...]
where the time goes in v3:
time: 57.5 us; the launch traced here: 57.3 us
  Pallas kernels  55.7 us (97%)
  local copies, waits for them, and re-layouts  1.57 us (3%)
    pallas_call x1, Pallas kernels, fused_device(): pl.pallas_call(functools.partial(kernel, n), out_shape=jax.ShapeDtypeStru...  55.7 us
    unnamed x1, local copies, waits for them, and re-layouts  1.57 us

profile of v3, /device:TPU:0, one launch (start us, length us, event | category | flops | bytes accessed | tf_op | source)
XLA Modules:
  0.0 57.3 jit_solution(17093012459949535821)
XLA Ops:
  0.0 55.7 %shard_map.64 = bf16[32,2048]{1,0:T(8,128)(2,1)} custom-call(bf16[32,2048]{1,0:T(8,128)(2,1)} %tokens.1, bf16[2048,4096]{1,0:T(8,128)(2,1)} %gate.1, bf16[2048,4096]{1,0:T(8,128)(2,1)} %up.1, bf16[4096,2048]{1,0:T(8,128)(2,1)} %down.1, s32[16,32]{1,0:T(8,128)} %in_mask.1, s32[16,32]{1,0:T(8,128)} %bitcast.1), custom_call_target="tpu_custom_call" | custom-call | flops 6442450944 | bytes 50331648 | tf_op jit(solution)/shard_map/pallas_call | solution.py:431
  55.7 1.6 %copy.8 = bf16[32,2048]{1,0:T(8,128)(2,1)} copy(bf16[32,2048]{1,0:T(8,128)(2,1)} %shard_map.64) | data formatting | bytes 262144

commit v4 on v2

--- a/solution.py
+++ b/solution.py
@@ -242,6 +242,9 @@
                     from_end(h, 0).start()
                     from_end(h, 1).start()
 
+        @pl.when(c == chunks - 1)
+        def _():
+            for h in range(halves):
                 to_mate(h).start()
 
     @pl.loop(0, chunks + 3)

time: 56.8 us -> 55.4 us (0.975)
  Pallas kernels: 55 us -> 53.6 us
    pallas_call x1, Pallas kernels: 55 us -> 53.6 us  [fused_device(): pl.pallas_call(functools.partial(kernel, n), out_shape=jax.ShapeDtypeStru...]
where the time goes in v4:
time: 55.4 us; the launch traced here: 55.2 us
  Pallas kernels  53.6 us (97%)
  local copies, waits for them, and re-layouts  1.57 us (3%)
    pallas_call x1, Pallas kernels, fused_device(): pl.pallas_call(functools.partial(kernel, n), out_shape=jax.ShapeDtypeStru...  53.6 us
    unnamed x1, local copies, waits for them, and re-layouts  1.57 us

profile of v4, /device:TPU:0, one launch (start us, length us, event | category | flops | bytes accessed | tf_op | source)
XLA Modules:
  0.0 55.2 jit_solution(17591690085109160359)
XLA Ops:
  0.0 53.6 %shard_map.64 = bf16[32,2048]{1,0:T(8,128)(2,1)} custom-call(bf16[32,2048]{1,0:T(8,128)(2,1)} %tokens.1, bf16[2048,4096]{1,0:T(8,128)(2,1)} %gate.1, bf16[2048,4096]{1,0:T(8,128)(2,1)} %up.1, bf16[4096,2048]{1,0:T(8,128)(2,1)} %down.1, s32[16,32]{1,0:T(8,128)} %in_mask.1, s32[16,32]{1,0:T(8,128)} %bitcast.1), custom_call_target="tpu_custom_call" | custom-call | flops 6442450944 | bytes 50331648 | tf_op jit(solution)/shard_map/pallas_call | solution.py:361
  53.6 1.6 %copy.8 = bf16[32,2048]{1,0:T(8,128)(2,1)} copy(bf16[32,2048]{1,0:T(8,128)(2,1)} %shard_map.64) | data formatting | bytes 262144
